TPU v7x, 32 devices: a whole 2x2x4 slice. The times are simulated.
32 devices in a mesh: grp: 2 (over x), ep: 16 (over z, y, core).
Axes of the slice: x: 2, y: 2, z: 4, core: 2. Of those that a mesh axis runs over, the one named last changes fastest.
Arguments:
- tokens: bfloat16 [2048, 2048], P(('grp', 'ep')), parts along dimension 0, may hold values from -6 to 6
- router_logits: float32 [2048, 8], P(('grp', 'ep')), parts along dimension 0, may hold values from -4 to 4
- expert_ids: int32 [2048, 8], P(('grp', 'ep')), parts along dimension 0, may hold values from 0 to 19, as said below
- gate_up: bfloat16 [16, 2048, 1536], P('ep'), may hold values from -0.125 to 0.125
- down: bfloat16 [16, 768, 2048], P('ep'), may hold values from -0.21875 to 0.21875
- hot_gate_up: bfloat16 [16, 2048, 384], P('ep'), may hold values from -0.125 to 0.125
- hot_down: bfloat16 [16, 192, 2048], P('ep'), may hold values from -0.21875 to 0.21875
- helper_list: int32 [16], replicated, may hold values from 0 to 15, as said below
Outputs:
- mixed: bfloat16 [2048, 2048], P(('grp', 'ep')), parts along dimension 0
There are 2 independent parts, one for each index of `grp`. A program takes and returns all parts, laid end to end along the dimension named above; an argument that names none is the same for every part. Nothing has to cross between parts.
Inputs may be any that keep to these rules, and one draw needn't show every extreme that they name: `expert_ids`: each row names 8 different experts; among the 64 tokens of one device every split expert is named by exactly 38 tokens and no owned expert by more than 38. `helper_list`: each device index appears once; the 4 devices of one split expert are an aligned block of 4 consecutive indices.
All inputs are finite; a program needn't handle non-finite values.
Results may differ from a plain program's by a relative error of at most 0.0058.
Values may be sent and summed in bfloat16 or wider, within the bound.
A program may use at most 128 MiB of HBM per device.

v0:
```python
import jax
import jax.numpy as jnp
from jax import lax
from jax.sharding import PartitionSpec as P

HELP = 4


def expert_partial(token_rows, gate_up_w, down_w):
    hidden_width = down_w.shape[0]
    projected = jnp.dot(token_rows, gate_up_w, preferred_element_type=jnp.float32)
    hidden = (jax.nn.silu(projected[:, :hidden_width]) * projected[:, hidden_width:]).astype(
        jnp.bfloat16
    )
    return jnp.dot(hidden, down_w, preferred_element_type=jnp.float32).astype(jnp.bfloat16)


def slot_picker(expert_ids, shares, targets, capacity):
    matches = expert_ids[:, :, None] == targets[None, None, :]
    factor = jnp.sum(jnp.where(matches, shares[:, :, None], jnp.float32(0.0)), axis=1)
    occupied = jnp.any(matches, axis=1)
    slot_index = jnp.cumsum(occupied.astype(jnp.int32), axis=0) - 1
    slot_ids = jnp.arange(capacity, dtype=jnp.int32)
    picker = occupied.T[:, None, :] & (slot_index.T[:, None, :] == slot_ids[None, :, None])
    weighted = jnp.where(picker, factor.T[:, None, :], jnp.float32(0.0))
    return (picker.astype(jnp.bfloat16), weighted)


def apply_expert(incoming, gate_up_w, down_w):
    layout = incoming.shape
    flattened = incoming.reshape(layout[0] * layout[1], layout[2])
    return expert_partial(flattened, gate_up_w, down_w).reshape(layout)


def per_device(
    tokens, router_logits, expert_ids, gate_up, down, hot_gate_up, hot_down, helper_list
):
    devices = lax.axis_size("ep")
    local_count = tokens.shape[0]
    top_count = expert_ids.shape[1]
    split_count = devices // HELP
    capacity = 3 * local_count * top_count // (2 * (devices + split_count))
    raised = jnp.exp(router_logits)
    shares = raised / jnp.sum(raised, axis=1, keepdims=True)
    device_ids = jnp.arange(devices, dtype=jnp.int32)
    position = jnp.sum(
        jnp.where(helper_list[None, :] == device_ids[:, None], device_ids[None, :], 0), axis=1
    )
    owner_pick, owner_weight = slot_picker(expert_ids, shares, device_ids, capacity)
    helper_pick, helper_weight = slot_picker(
        expert_ids, shares, devices + position // HELP, capacity
    )
    owner_send = jnp.einsum(
        "dct,tm->dcm", owner_pick, tokens, preferred_element_type=jnp.float32
    ).astype(jnp.bfloat16)
    helper_send = jnp.einsum(
        "dct,tm->dcm", helper_pick, tokens, preferred_element_type=jnp.float32
    ).astype(jnp.bfloat16)
    own_gate_up = gate_up[0]
    own_down = down[0]
    split_gate_up = hot_gate_up[0]
    split_down = hot_down[0]
    owner_in = lax.all_to_all(owner_send, "ep", split_axis=0, concat_axis=0, tiled=True)
    helper_in = lax.all_to_all(helper_send, "ep", split_axis=0, concat_axis=0, tiled=True)
    owner_out = apply_expert(owner_in, own_gate_up, own_down)
    helper_out = apply_expert(helper_in, split_gate_up, split_down)
    owner_back = lax.all_to_all(owner_out, "ep", split_axis=0, concat_axis=0, tiled=True)
    helper_back = lax.all_to_all(helper_out, "ep", split_axis=0, concat_axis=0, tiled=True)
    mixed = jnp.einsum(
        "dct,dcm->tm",
        owner_weight,
        owner_back,
        precision=lax.Precision.HIGHEST,
        preferred_element_type=jnp.float32,
    )
    mixed = mixed + jnp.einsum(
        "dct,dcm->tm",
        helper_weight,
        helper_back,
        precision=lax.Precision.HIGHEST,
        preferred_element_type=jnp.float32,
    )
    return mixed.astype(jnp.bfloat16)


def solution(mesh):
    return jax.shard_map(
        per_device,
        mesh=mesh,
        in_specs=(
            P(("grp", "ep"), None),
            P(("grp", "ep"), None),
            P(("grp", "ep"), None),
            P("ep", None, None),
            P("ep", None, None),
            P("ep", None, None),
            P("ep", None, None),
            P(),
        ),
        out_specs=P(("grp", "ep"), None),
        check_vma=False,
    )
```

profile of v0, /device:TPU:15, one launch (start us, length us, event | category | flops | bytes accessed | tf_op | source)
XLA Modules:
  0.0 265.9 jit_solution(730343864728762565)
XLA Ops:
  0.0 0.9 select_reduce_fusion.1
  0.9 0.8 compare_reduce_fusion
  1.8 0.1 reduce_window_sum.17
  2.0 3.3 %convolution_convert_fusion.1 = bf16[16,38,2048]{2,1,0:T(8,128)(2,1)} fusion(bf16[64,2048]{1,0:T(8,128)(2,1)} %param.8, s32[16,64]{1,0:T(8,128)S(1)} %copy.22, pred[16,64]{1,0:T(8,128)(4,1)S(1)} %bitcast.43), kind=kOutput, calls=%fused_computation.3 | convolution fusion | flops 160706560 | bytes 2757632 | tf_op jit(solution)/shard_map/dct,tm->dcm/dot_general | solution.py:53
  5.3 6.7 %all-to-all-start = ((bf16[16,38,2048]{2,1,0:T(8,128)(2,1)}), bf16[16,38,2048]{2,1,0:T(8,128)(2,1)}, u32[]{:S(2)}, u32[]{:S(2)}) async-start(bf16[16,38,2048]{2,1,0:T(8,128)(2,1)} %convolution_convert_fusion.1), calls=%async_computation | async-start | bytes 5242880 | tf_op jit(solution)/shard_map/all_to_all | solution.py:63
  12.1 0.1 reduce_window_sum.18
  12.3 2.3 convolution_convert_fusion
  14.6 56.2 %all-to-all-done = bf16[16,38,2048]{2,1,0:T(8,128)(2,1)} async-done(((bf16[16,38,2048]{2,1,0:T(8,128)(2,1)}), bf16[16,38,2048]{2,1,0:T(8,128)(2,1)}, u32[]{:S(2)}, u32[]{:S(2)}) %all-to-all-start) | async-done | bytes 2490400 | tf_op jit(solution)/shard_map/all_to_all | solution.py:63
  70.8 4.9 %all-to-all-start.2 = ((bf16[16,38,2048]{2,1,0:T(8,128)(2,1)}), bf16[16,38,2048]{2,1,0:T(8,128)(2,1)}, u32[]{:S(2)}, u32[]{:S(2)}) async-start(bf16[16,38,2048]{2,1,0:T(8,128)(2,1)} %convolution_convert_fusion), calls=%async_computation.2 | async-start | bytes 5242880 | tf_op jit(solution)/shard_map/all_to_all | solution.py:64
  75.7 4.3 %reshape.40 = bf16[608,2048]{1,0:T(8,128)(2,1)} reshape(bf16[16,38,2048]{2,1,0:T(8,128)(2,1)} %all-to-all-done) | data formatting | bytes 4980736 | tf_op jit(solution)/shard_map/reshape | solution.py:31
  79.9 6.9 %fusion = f32[608,1536]{1,0:T(8,128)S(1)} fusion(bf16[608,2048]{1,0:T(8,128)(2,1)} %reshape.40, bf16[1,2048,1536]{2,1,0:T(8,128)(2,1)} %param.11), kind=kOutput, calls=%fused_computation | convolution fusion | flops 3825205248 | bytes 12517376 | tf_op jit(solution)/shard_map/dot_general | solution.py:11
  86.8 3.6 %fusion.4 = bf16[608,2048]{1,0:T(8,128)(2,1)} fusion(bf16[1,768,2048]{2,1,0:T(8,128)(2,1)S(1)} %copy-done, f32[608,1536]{1,0:T(8,128)S(1)} %fusion), kind=kOutput, calls=%fused_computation.6 | convolution fusion | flops 1916649472 | bytes 9371648 | tf_op jit(solution)/shard_map/dot_general | solution.py:15
  90.5 4.2 %reshape.41 = bf16[16,38,2048]{2,1,0:T(8,128)(2,1)} reshape(bf16[608,2048]{1,0:T(8,128)(2,1)} %fusion.4) | data formatting | bytes 4980736 | tf_op jit(solution)/shard_map/reshape | solution.py:32
  94.7 39.7 %all-to-all-done.2 = bf16[16,38,2048]{2,1,0:T(8,128)(2,1)} async-done(((bf16[16,38,2048]{2,1,0:T(8,128)(2,1)}), bf16[16,38,2048]{2,1,0:T(8,128)(2,1)}, u32[]{:S(2)}, u32[]{:S(2)}) %all-to-all-start.2) | async-done | bytes 2490400 | tf_op jit(solution)/shard_map/all_to_all | solution.py:64
  134.4 4.9 %all-to-all-start.1 = ((bf16[16,38,2048]{2,1,0:T(8,128)(2,1)}), bf16[16,38,2048]{2,1,0:T(8,128)(2,1)}, u32[]{:S(2)}, u32[]{:S(2)}) async-start(bf16[16,38,2048]{2,1,0:T(8,128)(2,1)} %reshape.41), calls=%async_computation.1 | async-start | bytes 5242880 | tf_op jit(solution)/shard_map/all_to_all | solution.py:67
  139.3 4.3 %reshape.42 = bf16[608,2048]{1,0:T(8,128)(2,1)} reshape(bf16[16,38,2048]{2,1,0:T(8,128)(2,1)} %all-to-all-done.2) | data formatting | bytes 4980736 | tf_op jit(solution)/shard_map/reshape | solution.py:31
  143.6 3.7 %fusion.10 = f32[608,384]{1,0:T(8,128)S(1)} fusion(bf16[608,2048]{1,0:T(8,128)(2,1)} %reshape.42, bf16[1,2048,384]{2,1,0:T(8,128)(2,1)} %param.13), kind=kOutput, calls=%fused_computation.14 | convolution fusion | flops 956301312 | bytes 4997120 | tf_op jit(solution)/shard_map/dot_general | solution.py:11
  147.3 2.4 convolution_convert_fusion.2
  149.7 4.2 %reshape.43 = bf16[16,38,2048]{2,1,0:T(8,128)(2,1)} reshape(bf16[608,2048]{1,0:T(8,128)(2,1)} %convolution_convert_fusion.2) | data formatting | bytes 4980736 | tf_op jit(solution)/shard_map/reshape | solution.py:32
  153.9 44.2 %all-to-all-done.1 = bf16[16,38,2048]{2,1,0:T(8,128)(2,1)} async-done(((bf16[16,38,2048]{2,1,0:T(8,128)(2,1)}), bf16[16,38,2048]{2,1,0:T(8,128)(2,1)}, u32[]{:S(2)}, u32[]{:S(2)}) %all-to-all-start.1) | async-done | bytes 2490400 | tf_op jit(solution)/shard_map/all_to_all | solution.py:67
  198.1 4.9 %all-to-all-start.3 = ((bf16[16,38,2048]{2,1,0:T(8,128)(2,1)}), bf16[16,38,2048]{2,1,0:T(8,128)(2,1)}, u32[]{:S(2)}, u32[]{:S(2)}) async-start(bf16[16,38,2048]{2,1,0:T(8,128)(2,1)} %reshape.43), calls=%async_computation.3 | async-start | bytes 5242880 | tf_op jit(solution)/shard_map/all_to_all | solution.py:68
  203.1 4.1 %convolution_bitcast_fusion.1 = f32[64,2048]{1,0:T(8,128)} fusion(bf16[16,38,2048]{2,1,0:T(8,128)(2,1)} %all-to-all-done.1, f32[16,64]{1,0:T(8,128)S(1)} %bitcast.40, s32[16,64]{1,0:T(8,128)S(1)} %copy.22, pred[16,64]{1,0:T(8,128)(4,1)S(1)} %bitcast.44), kind=kOutput, calls=%fused_computation.10 | convolution fusion | flops 956418048 | bytes 3023872 | tf_op jit(solution)/shard_map/dct,dcm->tm/dot_general | solution.py:69
  207.3 54.5 %all-to-all-done.3 = bf16[16,38,2048]{2,1,0:T(8,128)(2,1)} async-done(((bf16[16,38,2048]{2,1,0:T(8,128)(2,1)}), bf16[16,38,2048]{2,1,0:T(8,128)(2,1)}, u32[]{:S(2)}, u32[]{:S(2)}) %all-to-all-start.3) | async-done | bytes 2490400 | tf_op jit(solution)/shard_map/all_to_all | solution.py:68
  261.8 4.1 %fusion.8 = bf16[64,2048]{1,0:T(8,128)(2,1)} fusion(f32[64,2048]{1,0:T(8,128)} %convolution_bitcast_fusion.1, bf16[16,38,2048]{2,1,0:T(8,128)(2,1)} %all-to-all-done.3, f32[16,64]{1,0:T(8,128)S(1)} %bitcast.39, s32[16,64]{1,0:T(8,128)S(1)} %copy.24, pred[16,64]{1,0:T(8,128)(4,1)S(1)} %bitcast.42), kind=kOutput, calls=%fused_computation.11 | convolution fusion | flops 956680192 | bytes 3286016 | tf_op jit(solution)/shard_map/dct,dcm->tm/dot_general | solution.py:76
  (22 shorter events, 0.5 us)
Async XLA Ops:
  0.0 86.8 %copy-start = (bf16[1,768,2048]{2,1,0:T(8,128)(2,1)S(1)}, bf16[1,768,2048]{2,1,0:T(8,128)(2,1)}, u32[]{:S(2)}) copy-start(bf16[1,768,2048]{2,1,0:T(8,128)(2,1)} %param.12) | copy-start | bytes 9437188
  5.3 6.9 %copy-start.1 = (bf16[64,2048]{1,0:T(8,128)(2,1)S(1)}, bf16[64,2048]{1,0:T(8,128)(2,1)}, u32[]{:S(2)}) copy-start(bf16[64,2048]{1,0:T(8,128)(2,1)} %param.8) | copy-start | bytes 786436
  5.3 65.4 %all-to-all-start = ((bf16[16,38,2048]{2,1,0:T(8,128)(2,1)}), bf16[16,38,2048]{2,1,0:T(8,128)(2,1)}, u32[]{:S(2)}, u32[]{:S(2)}) async-start(bf16[16,38,2048]{2,1,0:T(8,128)(2,1)} %convolution_convert_fusion.1), calls=%async_computation | async-start | bytes 5242880 | tf_op jit(solution)/shard_map/all_to_all | solution.py:63
  70.8 63.7 %all-to-all-start.2 = ((bf16[16,38,2048]{2,1,0:T(8,128)(2,1)}), bf16[16,38,2048]{2,1,0:T(8,128)(2,1)}, u32[]{:S(2)}, u32[]{:S(2)}) async-start(bf16[16,38,2048]{2,1,0:T(8,128)(2,1)} %convolution_convert_fusion), calls=%async_computation.2 | async-start | bytes 5242880 | tf_op jit(solution)/shard_map/all_to_all | solution.py:64
  134.4 63.7 %all-to-all-start.1 = ((bf16[16,38,2048]{2,1,0:T(8,128)(2,1)}), bf16[16,38,2048]{2,1,0:T(8,128)(2,1)}, u32[]{:S(2)}, u32[]{:S(2)}) async-start(bf16[16,38,2048]{2,1,0:T(8,128)(2,1)} %reshape.41), calls=%async_computation.1 | async-start | bytes 5242880 | tf_op jit(solution)/shard_map/all_to_all | solution.py:67
  143.6 3.7 %copy-start.4 = (bf16[1,192,2048]{2,1,0:T(8,128)(2,1)S(1)}, bf16[1,192,2048]{2,1,0:T(8,128)(2,1)}, u32[]{:S(2)}) copy-start(bf16[1,192,2048]{2,1,0:T(8,128)(2,1)} %param.14) | copy-start | bytes 2359300
  153.9 49.1 %copy-start.3 = (f32[64,8]{0,1:T(8,128)S(1)}, f32[64,8]{0,1:T(8,128)}, u32[]{:S(2)}) copy-start(f32[64,8]{0,1:T(8,128)} %param.9) | copy-start | bytes 6148
  153.9 49.1 %copy-start.2 = (s32[64,8]{0,1:T(8,128)S(1)}, s32[64,8]{0,1:T(8,128)}, u32[]{:S(2)}) copy-start(s32[64,8]{0,1:T(8,128)} %param.10) | copy-start | bytes 6148
  198.1 63.7 %all-to-all-start.3 = ((bf16[16,38,2048]{2,1,0:T(8,128)(2,1)}), bf16[16,38,2048]{2,1,0:T(8,128)(2,1)}, u32[]{:S(2)}, u32[]{:S(2)}) async-start(bf16[16,38,2048]{2,1,0:T(8,128)(2,1)} %reshape.43), calls=%async_computation.3 | async-start | bytes 5242880 | tf_op jit(solution)/shard_map/all_to_all | solution.py:68
where the time goes:
time: 267 us; the launch traced here: 266 us
  waiting for transfers between devices  195 us (73%)
  matrix products  30.5 us (11%)
  starting transfers between devices  21.4 us (8%)
  local copies, waits for them, and re-layouts  17.3 us (6%)
    all_to_all x1, waiting for transfers between devices, per_device(): lax.all_to_all(owner_send, 'ep', split_axis=0, concat_axis=0, tiled=True)  56.2 us
    all_to_all x1, waiting for transfers between devices, per_device(): lax.all_to_all(helper_out, 'ep', split_axis=0, concat_axis=0, tiled=True)  54.5 us
    all_to_all x1, waiting for transfers between devices, per_device(): lax.all_to_all(owner_out, 'ep', split_axis=0, concat_axis=0, tiled=True)  44.2 us
    all_to_all x1, waiting for transfers between devices, per_device(): lax.all_to_all(helper_send, 'ep', split_axis=0, concat_axis=0, tiled=True)  39.7 us
    dot_general x2, matrix products, expert_partial(): jnp.dot(token_rows, gate_up_w, preferred_element_type=jnp.float32)  10.5 us
    reshape x2, local copies, waits for them, and re-layouts, apply_expert(): flattened = incoming.reshape(layout[0] * layout[1], layout[2])  8.54 us
    reshape x2, local copies, waits for them, and re-layouts, apply_expert(): return expert_partial(flattened, gate_up_w, down_w).reshape(layout)  8.46 us
    all_to_all x1, starting transfers between devices, per_device(): lax.all_to_all(owner_send, 'ep', split_axis=0, concat_axis=0, tiled=True)  6.69 us
  transfers between devices with their start and end apart: 4, of which 4 were waited for; matrix products, arithmetic and copies ran while one was open for 15% of the time, Pallas kernels for 0%

commit v1 on v0

v1 whole, which is shorter than its diff:
```python
import jax
import jax.numpy as jnp
from jax import lax
from jax.sharding import PartitionSpec as P

HELP = 4


def per_device(
    tokens, router_logits, expert_ids, gate_up, down, hot_gate_up, hot_down, helper_list
):
    devices = lax.axis_size("ep")
    me = lax.axis_index("ep")
    experts = devices + devices // HELP
    raised = jnp.exp(router_logits)
    shares = raised / jnp.sum(raised, axis=1, keepdims=True)
    matches = expert_ids[:, :, None] == jnp.arange(experts, dtype=jnp.int32)[None, None, :]
    table = jnp.sum(jnp.where(matches, shares[:, :, None], jnp.float32(0.0)), axis=1)
    high = table.astype(jnp.bfloat16)
    low = (table - high.astype(jnp.float32)).astype(jnp.bfloat16)
    width = -(-2 * experts // 128) * 128
    extra = jnp.pad(jnp.concatenate([high, low], axis=1), ((0, 0), (0, width - 2 * experts)))
    sent = jnp.concatenate([tokens, extra], axis=1)
    rows = lax.all_gather(sent, "ep", axis=0, tiled=True)
    feature = tokens.shape[1]
    everyone = rows[:, :feature]
    tail = rows[:, feature:]
    split = devices + jnp.sum(
        jnp.where(helper_list == me, jnp.arange(devices, dtype=jnp.int32), 0)
    ) // HELP
    column = jnp.arange(width, dtype=jnp.int32)

    def factor(expert):
        chosen = (column == expert) | (column == expert + experts)
        return jnp.sum(
            jnp.where(chosen[None, :], tail.astype(jnp.float32), 0.0), axis=1, keepdims=True
        )

    def hidden(weights, share):
        projected = jnp.dot(everyone, weights, preferred_element_type=jnp.float32)
        half = weights.shape[1] // 2
        return (jax.nn.silu(projected[:, :half]) * projected[:, half:] * share).astype(
            jnp.bfloat16
        )

    partial = jnp.dot(hidden(gate_up[0], factor(me)), down[0], preferred_element_type=jnp.float32)
    partial = partial + jnp.dot(
        hidden(hot_gate_up[0], factor(split)), hot_down[0], preferred_element_type=jnp.float32
    )
    return lax.psum_scatter(
        partial.astype(jnp.bfloat16), "ep", scatter_dimension=0, tiled=True
    )


def solution(mesh):
    return jax.shard_map(
        per_device,
        mesh=mesh,
        in_specs=(
            P(("grp", "ep"), None),
            P(("grp", "ep"), None),
            P(("grp", "ep"), None),
            P("ep", None, None),
            P("ep", None, None),
            P("ep", None, None),
            P("ep", None, None),
            P(),
        ),
        out_specs=P(("grp", "ep"), None),
        check_vma=False,
    )
```

time: 267 us -> 163 us (0.61)
  the two profiles are of different devices: /device:TPU:15 before, /device:TPU:0 now
where the time goes in v1:
time: 163 us
  waiting for transfers between devices  122 us (75%)
  matrix products  19.1 us (12%)
  between operations  16.1 us (10%)
  other arithmetic  5.58 us (3%)
    reduce_scatter x1, waiting for transfers between devices, per_device(): lax.psum_scatter(partial.astype(jnp.bfloat16), 'ep', scatter_dimension=0,...  71 us
    all_gather x1, waiting for transfers between devices, per_device(): rows = lax.all_gather(sent, 'ep', axis=0, tiled=True)  50.9 us
    dot_general x2, matrix products, hidden(): projected = jnp.dot(everyone, weights, preferred_element_type=jnp.float32)  12 us
    dot_general x1, matrix products, per_device(): jnp.dot(hidden(gate_up[0], factor(me)), down[0], preferred_element_type=j...  3.81 us
  transfers between devices with their start and end apart: 2, of which 2 were waited for; matrix products, arithmetic and copies ran while one was open for 1% of the time, Pallas kernels for 0%

profile of v1, /device:TPU:0, one launch (start us, length us, event | category | flops | bytes accessed | tf_op | source)
XLA Modules:
  0.0 162.8 jit_solution(86338282056024633)
XLA Ops:
  6.5 0.0 copy-start
  6.5 0.0 all-gather.2.cloned.1.call-start
  6.5 0.9 exponential_reduce_fusion
  7.4 0.8 exponential_divide_fusion
  8.2 0.7 select_reduce_fusion
  8.9 0.1 copy.12
  9.0 1.7 %fusion.22 = bf16[64,2176]{1,0:T(8,128)(2,1)} fusion(bf16[64,40]{1,0:T(8,128)(2,1)S(1)} %copy.12, bf16[64,2048]{1,0:T(8,128)(2,1)} %param.8), kind=kLoop, calls=%fused_computation.26 | loop fusion | flops 835584 | bytes 545792 | tf_op jit(solution)/shard_map/concatenate | solution.py:23
  10.7 0.0 all-gather.2.cloned.1.call-update
  10.7 0.0 reduce-scatter.2.cloned.1.call-start
  10.8 1.3 fusion.23
  14.7 50.9 %all-gather.2.cloned.1.call-done = bf16[1024,2176]{1,0:T(8,128)(2,1)} async-done(((bf16[64,2176]{1,0:T(8,128)(2,1)}), bf16[1024,2176]{1,0:T(8,128)(2,1)}) %all-gather.2.cloned.1.call-update) | async-done | bytes 4456464 | tf_op jit(solution)/shard_map/all_gather | solution.py:24
  65.6 10.1 %fusion = f32[1024,1536]{1,0:T(8,128)S(1)} fusion(bf16[1,2048,1536]{2,1,0:T(8,128)(2,1)} %param.11, bf16[1024,2176]{1,0:T(8,128)(2,1)} %all-gather.2.cloned.1.call-done), kind=kOutput, calls=%fused_computation.1 | convolution fusion | flops 6442450944 | bytes 16777216 | tf_op jit(solution)/shard_map/dot_general | solution.py:40
  75.7 0.0 copy-done.2
  75.7 0.2 fusion.18
  75.9 0.0 copy-done
  76.0 0.0 copy-start.3
  76.0 3.8 %fusion.7 = f32[1024,2048]{1,0:T(8,128)S(1)} fusion(bf16[1,768,2048]{2,1,0:T(8,128)(2,1)S(1)} %copy-done, f32[1024,1536]{1,0:T(8,128)S(1)} %fusion, f32[1024]{0:T(1024)S(1)} %get-tuple-element.6), kind=kOutput, calls=%fused_computation.9 | convolution fusion | flops 3226730496 | bytes 17829888 | tf_op jit(solution)/shard_map/dot_general | solution.py:46
  79.8 0.0 copy-done.3
  79.8 0.0 copy-start.1
  79.8 1.9 %fusion.2 = f32[1024,384]{0,1:T(8,128)S(1)} fusion(bf16[1024,2176]{1,0:T(8,128)(2,1)S(1)} %copy-done.2, bf16[1,2048,384]{2,1,0:T(8,128)(2,1)S(1)} %copy-done.3), kind=kOutput, calls=%fused_computation.3 | convolution fusion | flops 1610612736 | bytes 7340032 | tf_op jit(solution)/shard_map/dot_general | solution.py:40
  81.7 0.0 copy-done.1
  81.7 3.3 %add_convert_fusion = bf16[1024,2048]{1,0:T(8,128)(2,1)} fusion(f32[1024,2048]{1,0:T(8,128)S(1)} %fusion.7, bf16[1,192,2048]{2,1,0:T(8,128)(2,1)S(1)} %copy-done.1, f32[1024,384]{0,1:T(8,128)S(1)} %fusion.2, f32[1024]{0:T(1024)S(1)} %get-tuple-element.5), kind=kOutput, calls=%fused_computation | convolution fusion | flops 810876928 | bytes 14946304 | tf_op jit(solution)/shard_map/dot_general | solution.py:47
  84.9 0.0 reduce-scatter.2.cloned.1.call-update
  85.0 71.0 %reduce-scatter.2.cloned.1.call-done = bf16[64,2048]{1,0:T(8,128)(2,1)} async-done(((bf16[1024,2048]{1,0:T(8,128)(2,1)}), bf16[64,2048]{1,0:T(8,128)(2,1)}) %reduce-scatter.2.cloned.1.call-update) | async-done | bytes 262160 | tf_op jit(solution)/shard_map/reduce_scatter | solution.py:50
  (4 shorter events, 0.0 us)
Async XLA Ops:
  6.5 69.4 %copy-start = (bf16[1,768,2048]{2,1,0:T(8,128)(2,1)S(1)}, bf16[1,768,2048]{2,1,0:T(8,128)(2,1)}, u32[]{:S(2)}) copy-start(bf16[1,768,2048]{2,1,0:T(8,128)(2,1)} %param.12) | copy-start | bytes 9437188
  6.5 59.0 %all-gather.2.cloned.1.call-start = ((), (), s32[]{:S(2)}) async-start(), calls=%async_computation.1 | async-start | bytes 4734976 | tf_op jit(solution)/shard_map/all_gather | solution.py:24
  10.7 145.2 %reduce-scatter.2.cloned.1.call-start = ((), (), s32[]{:S(2)}) async-start(), calls=%async_computation.2 | async-start | bytes 4456448 | tf_op jit(solution)/shard_map/reduce_scatter | solution.py:50
  65.6 10.1 %copy-start.2 = (bf16[1024,2176]{1,0:T(8,128)(2,1)S(1)}, bf16[1024,2176]{1,0:T(8,128)(2,1)}, u32[]{:S(2)}) copy-start(bf16[1024,2176]{1,0:T(8,128)(2,1)} %all-gather.2.cloned.1.call-done) | copy-start | bytes 13369348
  76.0 3.8 %copy-start.3 = (bf16[1,2048,384]{2,1,0:T(8,128)(2,1)S(1)}, bf16[1,2048,384]{2,1,0:T(8,128)(2,1)}, u32[]{:S(2)}) copy-start(bf16[1,2048,384]{2,1,0:T(8,128)(2,1)} %param.13) | copy-start | bytes 4718596
  79.8 1.9 %copy-start.1 = (bf16[1,192,2048]{2,1,0:T(8,128)(2,1)S(1)}, bf16[1,192,2048]{2,1,0:T(8,128)(2,1)}, u32[]{:S(2)}) copy-start(bf16[1,192,2048]{2,1,0:T(8,128)(2,1)} %param.14) | copy-start | bytes 2359300
Sparse Core Ops, SparseCore 0:
  10.9 54.6 all-gather.1
  85.1 70.8 reduce-scatter.1

commit v2 on v1

v2 whole, which is shorter than its diff:
```python
import functools

import jax
import jax.numpy as jnp
from jax import lax
from jax.experimental import pallas as pl
from jax.experimental.pallas import tpu as pltpu
from jax.sharding import PartitionSpec as P

HELP = 4
MESH = pl.DeviceIdType.MESH


def moe_kernel(
    devices,
    tokens_ref,
    logits_ref,
    ids_ref,
    helper_ref,
    gate_up_hbm,
    down_hbm,
    hot_gate_up_hbm,
    hot_down_hbm,
    out_ref,
    mine,
    rows_ref,
    core_in,
    side_in,
    rail_in,
    total,
    hidden_ref,
    gate_up_ref,
    hot_gate_up_ref,
    down_ref,
    weight_sem,
    send_sem,
    recv_sem,
):
    rails = devices // HELP
    count, feature = tokens_ref.shape
    width = mine.shape[1] - feature
    half = width // 2
    own_width = down_hbm.shape[1]
    hot_width = hot_down_hbm.shape[1]
    me = lax.axis_index("ep")
    rail = me // 4
    side = (me // 2) % 2
    core = me % 2

    def device(r, s, c):
        return {"ep": r * 4 + s * 2 + c}

    def plane(step):
        return lax.rem(rail + step, rails)

    core_peer = device(rail, side, 1 - core)
    side_peer = device(rail, 1 - side, core)
    kept = pl.multiple_of(core * (2 * count), 2 * count)
    given = pl.multiple_of((1 - core) * (2 * count), 2 * count)
    here = pl.multiple_of(core * (2 * count) + side * count, count)
    across = pl.multiple_of(core * (2 * count) + (1 - side) * count, count)
    whole = pl.ds(0, feature)

    def remote(src, dst, kind, step, target):
        return pltpu.make_async_remote_copy(
            src_ref=src,
            dst_ref=dst,
            send_sem=send_sem.at[kind, step],
            recv_sem=recv_sem.at[kind, step],
            device_id=target,
            device_id_type=MESH,
        )

    def gather_rail(step):
        return remote(
            mine,
            rows_ref.at[rail, pl.ds(here, count)],
            0,
            step,
            device(lax.rem(rail - step + rails, rails), side, core),
        )

    def gather_side(step):
        part = rows_ref.at[plane(step), pl.ds(here, count)]
        return remote(part, part, 1, step, side_peer)

    def gather_core(step):
        part = rows_ref.at[plane(step), pl.ds(kept, 2 * count)]
        return remote(part, part, 2, step, core_peer)

    def reduce_core(step):
        return remote(
            rows_ref.at[plane(step), pl.ds(given, 2 * count), whole],
            core_in.at[step],
            3,
            step,
            core_peer,
        )

    def reduce_side(step):
        return remote(
            rows_ref.at[plane(step), pl.ds(across, count), whole],
            side_in.at[step],
            4,
            step,
            side_peer,
        )

    def reduce_rail(step):
        return remote(
            rows_ref.at[plane(step), pl.ds(here, count), whole],
            rail_in.at[step],
            5,
            step,
            device(plane(step), side, core),
        )

    loads = [
        pltpu.make_async_copy(gate_up_hbm.at[0], gate_up_ref, weight_sem.at[0]),
        pltpu.make_async_copy(hot_gate_up_hbm.at[0], hot_gate_up_ref, weight_sem.at[1]),
        pltpu.make_async_copy(
            down_hbm.at[0], down_ref.at[pl.ds(0, own_width)], weight_sem.at[2]
        ),
        pltpu.make_async_copy(
            hot_down_hbm.at[0], down_ref.at[pl.ds(own_width, hot_width)], weight_sem.at[3]
        ),
    ]
    for load in loads:
        load.start()

    barrier = pltpu.get_barrier_semaphore()
    pl.semaphore_signal(barrier, inc=1, device_id=core_peer, device_id_type=MESH)
    pl.semaphore_signal(barrier, inc=1, device_id=side_peer, device_id_type=MESH)
    for step in range(1, rails):
        pl.semaphore_signal(
            barrier, inc=1, device_id=device(plane(step), side, core), device_id_type=MESH
        )

    raised = jnp.exp(logits_ref[...])
    shares = raised / jnp.sum(raised, axis=1, keepdims=True)
    chosen = ids_ref[...]
    column = lax.broadcasted_iota(jnp.int32, (count, width), 1)
    expert = jnp.where(column < half, column, column - half)
    table = jnp.zeros((count, width), jnp.float32)
    for k in range(chosen.shape[1]):
        table = table + jnp.where(expert == chosen[:, k : k + 1], shares[:, k : k + 1], 0.0)
    high = table.astype(jnp.bfloat16).astype(jnp.float32)
    table = jnp.where(column < half, high, table - high).astype(jnp.bfloat16)
    held = tokens_ref[...]
    mine[:, pl.ds(0, feature)] = held
    mine[:, pl.ds(feature, width)] = table
    rows_ref[rail, pl.ds(here, count), pl.ds(0, feature)] = held
    rows_ref[rail, pl.ds(here, count), pl.ds(feature, width)] = table

    helper = helper_ref[...]
    entry = lax.broadcasted_iota(jnp.int32, helper.shape, 1)
    position = jnp.sum(jnp.where(helper == me, entry, 0), axis=1, keepdims=True)
    split = devices + position // HELP

    pl.semaphore_wait(barrier, rails + 1)
    gather_side(0).start()
    for step in range(1, rails):
        gather_rail(step).start()

    def to_side(step):
        reduce_core(step).wait_recv()
        at = plane(step)
        theirs = pl.ds(pl.multiple_of((1 - side) * count, count), count)
        rows_ref[at, pl.ds(across, count), whole] = (
            rows_ref[at, pl.ds(across, count), whole].astype(jnp.float32)
            + core_in[step, theirs, :].astype(jnp.float32)
        ).astype(jnp.bfloat16)
        reduce_side(step).start()

    def plane_sum(step):
        reduce_side(step).wait_recv()
        ours = pl.ds(pl.multiple_of(side * count, count), count)
        return (
            rows_ref[plane(step), pl.ds(here, count), whole].astype(jnp.float32)
            + core_in[step, ours, :].astype(jnp.float32)
            + side_in[step].astype(jnp.float32)
        )

    def to_rail(step):
        rows_ref[plane(step), pl.ds(here, count), whole] = plane_sum(step).astype(jnp.bfloat16)
        reduce_rail(step).start()

    def stage(step, carry):
        at = plane(step)

        @pl.when(step + 1 < rails)
        def _():
            gather_rail(step + 1).wait_recv()
            gather_side(step + 1).start()

        gather_side(step).wait_recv()
        gather_core(step).start()

        @pl.when(step == 0)
        def _():
            for load in loads[:2]:
                load.wait()

        gather_core(step).wait_recv()
        tokens = rows_ref[at, :, pl.ds(0, feature)]
        tail = rows_ref[at, :, pl.ds(feature, width)].astype(jnp.float32)
        lane = lax.broadcasted_iota(jnp.int32, (1, width), 1)
        lane = jnp.where(lane < half, lane, lane - half)
        own_share = jnp.sum(jnp.where(lane == me, tail, 0.0), axis=1, keepdims=True)
        hot_share = jnp.sum(jnp.where(lane == split, tail, 0.0), axis=1, keepdims=True)
        tile = 256
        for at_column in range(0, own_width, tile):
            gate = jnp.dot(
                tokens,
                gate_up_ref[:, pl.ds(at_column, tile)],
                preferred_element_type=jnp.float32,
            )
            up = jnp.dot(
                tokens,
                gate_up_ref[:, pl.ds(own_width + at_column, tile)],
                preferred_element_type=jnp.float32,
            )
            hidden_ref[:, pl.ds(at_column, tile)] = (
                jax.nn.silu(gate) * up * own_share
            ).astype(jnp.bfloat16)
        both = jnp.dot(tokens, hot_gate_up_ref[...], preferred_element_type=jnp.float32)
        hidden_ref[:, pl.ds(own_width, hot_width)] = (
            jax.nn.silu(both[:, :hot_width]) * both[:, hot_width:] * hot_share
        ).astype(jnp.bfloat16)

        @pl.when(step >= 1)
        def _():
            to_side(step - 1)

        @pl.when(step >= 3)
        def _():
            to_rail(step - 2)

        @pl.when(step == 2)
        def _():
            total[...] = plane_sum(0)

        @pl.when(step == 0)
        def _():
            for load in loads[2:]:
                load.wait()

        gather_side(step).wait_send()
        gather_core(step).wait_send()
        hidden = hidden_ref[...]
        for at_column in range(0, feature, 512):
            rows_ref[at, :, pl.ds(at_column, 512)] = jnp.dot(
                hidden,
                down_ref[:, pl.ds(at_column, 512)],
                preferred_element_type=jnp.float32,
            ).astype(jnp.bfloat16)
        reduce_core(step).start()
        return carry

    lax.fori_loop(0, rails, stage, 0)
    to_side(rails - 1)
    to_rail(rails - 2)
    to_rail(rails - 1)
    result = total[...]
    for step in range(1, rails):
        reduce_rail(step).wait_recv()
        result = result + rail_in[step].astype(jnp.float32)
    out_ref[...] = result.astype(jnp.bfloat16)
    for step in range(rails):
        reduce_core(step).wait_send()
        reduce_side(step).wait_send()
        if step:
            gather_rail(step).wait_send()
            reduce_rail(step).wait_send()


def per_device(
    tokens, router_logits, expert_ids, gate_up, down, hot_gate_up, hot_down, helper_list
):
    devices = lax.axis_size("ep")
    rails = devices // HELP
    count, feature = tokens.shape
    experts = devices + rails
    half = -(-experts // 64) * 64
    width = 2 * half
    hidden = down.shape[1] + hot_down.shape[1]
    bf16 = jnp.bfloat16
    vmem = pl.BlockSpec(memory_space=pltpu.VMEM)
    hbm = pl.BlockSpec(memory_space=pl.ANY)
    return pl.pallas_call(
        functools.partial(moe_kernel, devices),
        out_shape=jax.ShapeDtypeStruct((count, feature), bf16),
        in_specs=[vmem] * 4 + [hbm] * 4,
        out_specs=vmem,
        scratch_shapes=[
            pltpu.VMEM((count, feature + width), bf16),
            pltpu.VMEM((rails, HELP * count, feature + width), bf16),
            pltpu.VMEM((rails, 2 * count, feature), bf16),
            pltpu.VMEM((rails, count, feature), bf16),
            pltpu.VMEM((rails, count, feature), bf16),
            pltpu.VMEM((count, feature), jnp.float32),
            pltpu.VMEM((HELP * count, hidden), bf16),
            pltpu.VMEM(gate_up.shape[1:], bf16),
            pltpu.VMEM(hot_gate_up.shape[1:], bf16),
            pltpu.VMEM((hidden, feature), bf16),
            pltpu.SemaphoreType.DMA((4,)),
            pltpu.SemaphoreType.DMA((6, rails)),
            pltpu.SemaphoreType.DMA((6, rails)),
        ],
        compiler_params=pltpu.CompilerParams(
            collective_id=0, has_side_effects=True, vmem_limit_bytes=60 * 1024 * 1024
        ),
    )(
        tokens,
        router_logits,
        expert_ids,
        helper_list.reshape(1, devices),
        gate_up,
        down,
        hot_gate_up,
        hot_down,
    )


def solution(mesh):
    return jax.shard_map(
        per_device,
        mesh=mesh,
        in_specs=(
            P(("grp", "ep"), None),
            P(("grp", "ep"), None),
            P(("grp", "ep"), None),
            P("ep", None, None),
            P("ep", None, None),
            P("ep", None, None),
            P("ep", None, None),
            P(),
        ),
        out_specs=P(("grp", "ep"), None),
        check_vma=False,
    )
```

time: 163 us -> 83.5 us (0.51)
  the two profiles are of different devices: /device:TPU:0 before, /device:TPU:25 now
where the time goes in v2:
time: 83.5 us; the launch traced here: 83.2 us
  Pallas kernels  78.8 us (94%)
  local copies, waits for them, and re-layouts  4.42 us (5%)
    pallas_call x1, Pallas kernels, per_device(): pl.pallas_call(functools.partial(moe_kernel, devices), out_shape=jax.Shap...  78.8 us
    unnamed x3, local copies, waits for them, and re-layouts  4.42 us

profile of v2, /device:TPU:25, one launch (start us, length us, event | category | flops | bytes accessed | tf_op | source)
XLA Modules:
  0.0 83.2 jit_solution(17241846529176427855)
XLA Ops:
  0.0 1.4 %copy.9.logits_ref = f32[64,8]{1,0:T(8,128)} copy(f32[64,8]{0,1:T(8,128)} %param.9) | data formatting | bytes 4096 | tf_op args[1]
  1.4 1.4 %copy.10.ids_ref = s32[64,8]{1,0:T(8,128)} copy(s32[64,8]{0,1:T(8,128)} %param.10) | data formatting | bytes 4096 | tf_op args[2]
  2.8 78.8 %shard_map.82 = bf16[64,2048]{1,0:T(8,128)(2,1)} custom-call(bf16[64,2048]{1,0:T(8,128)(2,1)} %tokens_ref.1, f32[64,8]{1,0:T(8,128)} %copy.9.logits_ref, s32[64,8]{1,0:T(8,128)} %copy.10.ids_ref, s32[1,16]{1,0:T(1,128)} %bitcast.1, bf16[1,2048,1536]{2,1,0:T(8,128)(2,1)} %gate_up_hbm.1, bf16[1,768,2048]{2,1,0:T(8,128)(2,1)} %down_hbm.1, ...), custom_call_target="tpu_custom_call" | custom-call | tf_op jit(solution)/shard_map/pallas_call | solution.py:290
  81.6 1.7 %copy.12 = bf16[64,2048]{1,0:T(8,128)(2,1)} copy(bf16[64,2048]{1,0:T(8,128)(2,1)} %shard_map.82) | data formatting | bytes 524288

commit v3 on v2

--- a/solution.py
+++ b/solution.py
@@ -27,7 +27,6 @@
     core_in,
     side_in,
     rail_in,
-    total,
     hidden_ref,
     gate_up_ref,
     hot_gate_up_ref,
@@ -51,7 +50,13 @@
         return {"ep": r * 4 + s * 2 + c}
 
     def plane(step):
-        return lax.rem(rail + step, rails)
+        offset = jnp.where(step < 2, step, rails + 1 - step)
+        partner = 0
+        bit = 1
+        while bit < rails:
+            partner = partner + bit * ((rail // bit + offset // bit) % 2)
+            bit *= 2
+        return partner
 
     core_peer = device(rail, side, 1 - core)
     side_peer = device(rail, 1 - side, core)
@@ -77,7 +82,7 @@
             rows_ref.at[rail, pl.ds(here, count)],
             0,
             step,
-            device(lax.rem(rail - step + rails, rails), side, core),
+            device(plane(step), side, core),
         )
 
     def gather_side(step):
@@ -159,8 +164,8 @@
 
     pl.semaphore_wait(barrier, rails + 1)
     gather_side(0).start()
-    for step in range(1, rails):
-        gather_rail(step).start()
+    gather_rail(1).start()
+    gather_rail(2).start()
 
     def to_side(step):
         reduce_core(step).wait_recv()
@@ -185,18 +190,31 @@
         rows_ref[plane(step), pl.ds(here, count), whole] = plane_sum(step).astype(jnp.bfloat16)
         reduce_rail(step).start()
 
-    def stage(step, carry):
+    gather_rail(1).wait_recv()
+    gather_side(1).start()
+    gather_side(0).wait_recv()
+    gather_core(0).start()
+
+    def stage(index, carry):
+        step = lax.rem(index + 1, rails)
         at = plane(step)
 
-        @pl.when(step + 1 < rails)
-        def _():
-            gather_rail(step + 1).wait_recv()
-            gather_side(step + 1).start()
-
-        gather_side(step).wait_recv()
-        gather_core(step).start()
-
-        @pl.when(step == 0)
+        def next_rail():
+            gather_rail(index + 2).wait_recv()
+            gather_side(index + 2).start()
+
+            @pl.when(index + 3 < rails)
+            def _():
+                gather_rail(index + 3).start()
+
+        pl.when(index + 3 < rails)(next_rail)
+
+        @pl.when(step > 0)
+        def _():
+            gather_side(step).wait_recv()
+            gather_core(step).start()
+
+        @pl.when(index == 0)
         def _():
             for load in loads[:2]:
                 load.wait()
@@ -228,19 +246,17 @@
             jax.nn.silu(both[:, :hot_width]) * both[:, hot_width:] * hot_share
         ).astype(jnp.bfloat16)
 
-        @pl.when(step >= 1)
-        def _():
-            to_side(step - 1)
-
-        @pl.when(step >= 3)
-        def _():
-            to_rail(step - 2)
-
-        @pl.when(step == 2)
-        def _():
-            total[...] = plane_sum(0)
-
-        @pl.when(step == 0)
+        pl.when(index + 3 == rails)(next_rail)
+
+        @pl.when(index >= 1)
+        def _():
+            to_side(index)
+
+        @pl.when(index >= 2)
+        def _():
+            to_rail(index - 1)
+
+        @pl.when(index == 0)
         def _():
             for load in loads[2:]:
                 load.wait()
@@ -258,10 +274,9 @@
         return carry
 
     lax.fori_loop(0, rails, stage, 0)
-    to_side(rails - 1)
-    to_rail(rails - 2)
     to_rail(rails - 1)
-    result = total[...]
+    to_side(0)
+    result = plane_sum(0)
     for step in range(1, rails):
         reduce_rail(step).wait_recv()
         result = result + rail_in[step].astype(jnp.float32)
@@ -298,7 +313,6 @@
             pltpu.VMEM((rails, 2 * count, feature), bf16),
             pltpu.VMEM((rails, count, feature), bf16),
             pltpu.VMEM((rails, count, feature), bf16),
-            pltpu.VMEM((count, feature), jnp.float32),
             pltpu.VMEM((HELP * count, hidden), bf16),
             pltpu.VMEM(gate_up.shape[1:], bf16),
             pltpu.VMEM(hot_gate_up.shape[1:], bf16),

time: 83.5 us -> 81.2 us (0.972)
  the two profiles are of different devices: /device:TPU:25 before, /device:TPU:0 now
where the time goes in v3:
time: 81.2 us; the launch traced here: 80.4 us
  Pallas kernels  76 us (94%)
  local copies, waits for them, and re-layouts  4.42 us (5%)
    pallas_call x1, Pallas kernels, per_device(): pl.pallas_call(functools.partial(moe_kernel, devices), out_shape=jax.Shap...  76 us
    unnamed x3, local copies, waits for them, and re-layouts  4.42 us

profile of v3, /device:TPU:0, one launch (start us, length us, event | category | flops | bytes accessed | tf_op | source)
XLA Modules:
  0.0 80.4 jit_solution(13385405710963385027)
XLA Ops:
  0.0 1.4 %copy.9.logits_ref = f32[64,8]{1,0:T(8,128)} copy(f32[64,8]{0,1:T(8,128)} %param.9) | data formatting | bytes 4096 | tf_op args[1]
  1.4 1.4 %copy.10.ids_ref = s32[64,8]{1,0:T(8,128)} copy(s32[64,8]{0,1:T(8,128)} %param.10) | data formatting | bytes 4096 | tf_op args[2]
  2.8 76.0 %shard_map.82 = bf16[64,2048]{1,0:T(8,128)(2,1)} custom-call(bf16[64,2048]{1,0:T(8,128)(2,1)} %tokens_ref.1, f32[64,8]{1,0:T(8,128)} %copy.9.logits_ref, s32[64,8]{1,0:T(8,128)} %copy.10.ids_ref, s32[1,16]{1,0:T(1,128)} %bitcast.1, bf16[1,2048,1536]{2,1,0:T(8,128)(2,1)} %gate_up_hbm.1, bf16[1,768,2048]{2,1,0:T(8,128)(2,1)} %down_hbm.1, ...), custom_call_target="tpu_custom_call" | custom-call | tf_op jit(solution)/shard_map/pallas_call | solution.py:305
  78.8 1.7 %copy.12 = bf16[64,2048]{1,0:T(8,128)(2,1)} copy(bf16[64,2048]{1,0:T(8,128)(2,1)} %shard_map.82) | data formatting | bytes 524288

commit v4 on v3

--- a/solution.py
+++ b/solution.py
@@ -214,6 +214,10 @@
             gather_side(step).wait_recv()
             gather_core(step).start()
 
+        @pl.when(index >= 1)
+        def _():
+            to_side(index)
+
         @pl.when(index == 0)
         def _():
             for load in loads[:2]:
@@ -248,14 +252,6 @@
 
         pl.when(index + 3 == rails)(next_rail)
 
-        @pl.when(index >= 1)
-        def _():
-            to_side(index)
-
-        @pl.when(index >= 2)
-        def _():
-            to_rail(index - 1)
-
         @pl.when(index == 0)
         def _():
             for load in loads[2:]:
@@ -271,10 +267,14 @@
                 preferred_element_type=jnp.float32,
             ).astype(jnp.bfloat16)
         reduce_core(step).start()
+
+        @pl.when(index >= 1)
+        def _():
+            to_rail(index)
+
         return carry
 
     lax.fori_loop(0, rails, stage, 0)
-    to_rail(rails - 1)
     to_side(0)
     result = plane_sum(0)
     for step in range(1, rails):

time: 81.2 us -> 77.2 us (0.951)
  Pallas kernels: 76 us -> 72.6 us
    pallas_call x1, Pallas kernels: 76 us -> 72.6 us  [per_device(): pl.pallas_call(functools.partial(moe_kernel, devices), out_shape=jax.Shap...]
where the time goes in v4:
time: 77.2 us; the launch traced here: 77 us
  Pallas kernels  72.6 us (94%)
  local copies, waits for them, and re-layouts  4.42 us (6%)
    pallas_call x1, Pallas kernels, per_device(): pl.pallas_call(functools.partial(moe_kernel, devices), out_shape=jax.Shap...  72.6 us
    unnamed x3, local copies, waits for them, and re-layouts  4.42 us

profile of v4, /device:TPU:0, one launch (start us, length us, event | category | flops | bytes accessed | tf_op | source)
XLA Modules:
  0.0 77.0 jit_solution(5742148483607176526)
XLA Ops:
  0.0 1.4 %copy.9.logits_ref = f32[64,8]{1,0:T(8,128)} copy(f32[64,8]{0,1:T(8,128)} %param.9) | data formatting | bytes 4096 | tf_op args[1]
  1.4 1.4 %copy.10.ids_ref = s32[64,8]{1,0:T(8,128)} copy(s32[64,8]{0,1:T(8,128)} %param.10) | data formatting | bytes 4096 | tf_op args[2]
  2.8 72.6 %shard_map.82 = bf16[64,2048]{1,0:T(8,128)(2,1)} custom-call(bf16[64,2048]{1,0:T(8,128)(2,1)} %tokens_ref.1, f32[64,8]{1,0:T(8,128)} %copy.9.logits_ref, s32[64,8]{1,0:T(8,128)} %copy.10.ids_ref, s32[1,16]{1,0:T(1,128)} %bitcast.1, bf16[1,2048,1536]{2,1,0:T(8,128)(2,1)} %gate_up_hbm.1, bf16[1,768,2048]{2,1,0:T(8,128)(2,1)} %down_hbm.1, ...), custom_call_target="tpu_custom_call" | custom-call | tf_op jit(solution)/shard_map/pallas_call | solution.py:305
  75.3 1.7 %copy.12 = bf16[64,2048]{1,0:T(8,128)(2,1)} copy(bf16[64,2048]{1,0:T(8,128)(2,1)} %shard_map.82) | data formatting | bytes 524288
